TPU v7x, 256 devices: a whole 4x4x8 slice. The times are simulated.
256 devices in a mesh: ka: 64 (over x, z_lo, y), aux: 4 (over z_hi, core).
Axes of the slice: x: 4, y: 4, z: 8 (z_hi: 2, z_lo: 4; z = z_hi * 4 + z_lo), core: 2. Of those that a mesh axis runs over, the one named last changes fastest.
Arguments:
- lambda_blocks: bfloat16 [64, 8, 16, 64, 64], P('ka', None, 'aux'), may hold values from -6 to 6
- left_tiles: bfloat16 [64, 2, 256, 64, 64], P('ka', None, 'aux'), may hold values from -0.1875 to 0.1875
- right_tiles: bfloat16 [64, 2, 256, 64, 64], P('ka', None, 'aux'), may hold values from -0.1875 to 0.1875
Outputs:
- ladder: float32 [64, 8, 16, 64, 64], P('ka', None, 'aux')
All inputs are finite; a program needn't handle non-finite values.
Results may differ from a plain program's by a relative error of at most 0.0029.
Values may be sent and summed in bfloat16 or wider, within the bound.
No kernel may reach another device: no remote copies, remote signals or barrier semaphores. Data moves between devices by JAX's collectives and lax.ppermute only.
A program may use at most 64 MiB of HBM per device.

v0:
```python
import functools

import jax
import jax.numpy as jnp
from jax import lax
from jax.experimental import pallas as pl
from jax.experimental.pallas import tpu as pltpu
from jax.sharding import PartitionSpec as P

BF16 = jnp.bfloat16
F32 = jnp.float32
VMEM = pl.BlockSpec(memory_space=pltpu.VMEM)
SMEM = pl.BlockSpec(memory_space=pltpu.SMEM)
ANY = pl.BlockSpec(memory_space=pl.ANY)
MIB = 2**20


def params(mib, **kw):
    return pltpu.CompilerParams(vmem_limit_bytes=mib * MIB, **kw)


def spread(src, dst, held, count, swap, unroll):
    def put(n, _):
        x = src[n].T if swap else src[n]
        rows = pl.ds(pl.multiple_of(n * 32, 32), 32)
        held[rows, :] = jnp.concatenate([x[:32], x[32:]], axis=1).astype(F32)
        return 0

    lax.fori_loop(0, count, put, 0, unroll=unroll)
    for ref, first in dst:
        take(ref, held, first, count)


def take(dst, held, first, count):
    for t in range(dst.shape[1] // 128):
        dst[:, t * 128 : (t + 1) * 128] = held[pl.ds(first + t, count, stride=32), :].astype(BF16)


def in_hbm(x):
    return pltpu.with_memory_space_constraint(x, pltpu.HBM)


def in_vmem(x):
    return pltpu.with_memory_space_constraint(x, pltpu.VMEM)


def cost(flops, mib):
    return pl.CostEstimate(flops=flops // 1000, bytes_accessed=int(mib * 1024), transcendentals=0)


def lambda_kernel(lam, out, again, held):
    spread(lam, [(out, 0)], held, lam.shape[0], True, 32)
    again[...] = out[...]


def flat_lambda(lam):
    n = lam.shape[0]
    flat = pl.BlockSpec((n, 4096), lambda i: (0, 0))
    return pl.pallas_call(
        lambda_kernel,
        grid=(1,),
        out_shape=[jax.ShapeDtypeStruct((n, 4096), BF16)] * 2,
        in_specs=[pl.BlockSpec((n, 64, 64), lambda i: (0, 0, 0))],
        out_specs=[flat] * 2,
        scratch_shapes=[pltpu.VMEM((n * 32, 128), F32)],
        compiler_params=params(8),
        cost_estimate=cost(0, 6),
        name="flat_lambda",
    )(in_hbm(lam))


def factor_kernel(core, left, right, done, mine, sent, held_l, held_r):
    half = core[0]
    spread(left.at[0], [(mine, half * 16), (sent.at[:, :2048], (1 - half) * 16)], held_l, 32, False, 32)
    spread(right.at[0], [(sent.at[:, 2048:], 0)], held_r, 32, True, 32)


def flat_factors(core, left, right, s, done):
    block = pl.BlockSpec((1, 32, 64, 64), lambda i: (s, i, 0, 0))
    return pl.pallas_call(
        factor_kernel,
        grid=(2,),
        out_shape=[jax.ShapeDtypeStruct((64, n), BF16) for n in (2048, 6144)],
        in_specs=[SMEM, block, block, ANY],
        out_specs=[pl.BlockSpec((32, n), lambda i: (i, 0)) for n in (2048, 6144)],
        scratch_shapes=[pltpu.VMEM((32 * 32, 128), F32)] * 2,
        compiler_params=params(8),
        cost_estimate=cost(0, 400000),
        name="flat_factors",
    )(core, in_hbm(left), in_hbm(right), done)


TS = 4
HALF = 16


def build_kernel(first, mine, sent, got_here, done, w, x, s):
    for ap in range(16):
        at = slice(ap * 128, (ap + 1) * 128)
        v = jnp.concatenate([mine[:, at], got_here[:, at]], axis=0).T
        x[ap * 64 : (ap + 1) * 64, :] = jnp.concatenate([v[:64], v[64:]], axis=1)
    low = lax.broadcasted_iota(jnp.int32, (128, 128), 1) < 64
    zero = jnp.zeros((128, 128), BF16)

    def fill(slot, u):
        for i in range(TS):
            t = first + jnp.minimum(u * TS + i, HALF - 1)
            at = pl.ds(pl.multiple_of(2048 + t * 128, 128), 128)
            v = jnp.concatenate([sent[:, at], got_here[:, at]], axis=0)
            r = jnp.concatenate([v[:, 64:], v[:, :64]], axis=1)
            a, b = i * 256, i * 256 + 128
            s[slot, 0:128, a : a + 128] = jnp.where(low, v, zero)
            s[slot, 0:128, b : b + 128] = jnp.where(low, r, zero)
            s[slot, 128:256, a : a + 128] = jnp.where(low, zero, r)
            s[slot, 128:256, b : b + 128] = jnp.where(low, zero, v)

    def work(u, slot):
        fill(1 - slot, u + 1)
        for m in range(8):
            got = jnp.dot(x[m * 128 : (m + 1) * 128, :], s[slot], preferred_element_type=F32).astype(BF16)
            for i in range(TS * 2):
                at = pl.ds(pl.multiple_of((u * TS * 2 + i) * 64, 64), 64)
                for p in range(2):
                    w[at, (m * 2 + p) * 128 : (m * 2 + p + 1) * 128] = got[
                        p * 64 : (p + 1) * 64, i * 128 : (i + 1) * 128
                    ]

    def pair(v, _):
        work(v * 2, 0)
        work(v * 2 + 1, 1)
        return 0

    fill(0, 0)
    lax.fori_loop(0, HALF // TS // 2, pair, 0)


def build(first, mine, sent, got, done, weight=1):
    return pl.pallas_call(
        functools.partial(build_kernel, first),
        out_shape=pltpu.VMEM((HALF * 128, 2048), BF16),
        in_specs=[VMEM] * 3 + [ANY],
        out_specs=VMEM,
        scratch_shapes=[pltpu.VMEM((1024, 256), BF16), pltpu.VMEM((2, 256, 256 * TS), BF16)],
        compiler_params=params(6),
        cost_estimate=cost(2 * 1024 * 256 * 4096 * weight, 9 * weight),
        name="build_w",
    )(mine, sent, got, done)


def contract_kernel(last, first, *refs):
    n_out = 4 if last else 1
    pieces, ws, so_far, outs, (lhs, sems) = refs[:4], refs[4:6], refs[6:-2 - n_out], refs[-2 - n_out : -2], refs[-2:]
    copies = []
    for p, piece in enumerate(pieces):
        copies.append(pltpu.make_async_copy(piece, lhs.at[pl.ds(p * 32, 32)], sems.at[p]))
    for c in copies:
        c.start()
    for c in copies:
        c.wait()
    width = 512
    deep = HALF * 128
    for n in range(outs[0].shape[1] // width):
        at = slice(n * width, (n + 1) * width)
        src = slice(first + n * width, first + (n + 1) * width)
        got = jnp.dot(lhs[:, :deep], ws[0][:, src], preferred_element_type=F32)
        got += jnp.dot(lhs[:, deep:], ws[1][:, src], preferred_element_type=F32)
        if last:
            got += so_far[0][:, src]
            own, core, zed, diag = outs
            own[:, at] = got[0:32]
            core[:, at] = got[32:64]
            zed[:, at] = got[64:96].astype(BF16)
            diag[:, at] = got[96:128].astype(BF16)
        else:
            outs[0][:, at] = got


def contract(pieces, ws, so_far=None, first=0, cols=2048):
    last = so_far is not None
    rows = ((32, F32), (32, F32), (32, BF16), (32, BF16)) if last else ((128, F32),)
    return pl.pallas_call(
        functools.partial(contract_kernel, last, first),
        out_shape=[jax.ShapeDtypeStruct((r, cols), t) for r, t in rows],
        in_specs=[ANY] * 4 + [VMEM] * (2 + last),
        out_specs=[VMEM] * len(rows),
        scratch_shapes=[pltpu.VMEM((128, 4096), BF16), pltpu.SemaphoreType.DMA((4,))],
        compiler_params=params(8),
        cost_estimate=cost(2 * 128 * 4096 * 2048, 12),
        name="contract",
    )(*pieces, *(in_vmem(w) for w in ws), *((so_far,) if last else ()))


def finish_kernel(core, *refs):
    parts, out, held = refs[:-2], refs[-2], refs[-1]
    half = core[0]
    per = 16
    for ap in range(16):
        own, zed, other, diag = parts[ap // per * 4 : ap // per * 4 + 4]
        at = slice(ap % per * 128, (ap % per + 1) * 128)
        held[pl.ds(half * 16 + ap, 32, stride=32), :] = own[:, at] + zed[:, at].astype(F32)
        held[pl.ds((1 - half) * 16 + ap, 32, stride=32), :] = other[:, at] + diag[:, at].astype(F32)

    def put(n, _):
        x = held[pl.ds(pl.multiple_of(n * 32, 32), 32), :]
        out[n, 0:32, :] = x[:, :64]
        out[n, 32:64, :] = x[:, 64:]
        return 0

    lax.fori_loop(0, 32, put, 0, unroll=16)


def finish(core, parts):
    return pl.pallas_call(
        finish_kernel,
        out_shape=jax.ShapeDtypeStruct((32, 64, 64), F32),
        in_specs=[SMEM] + [VMEM] * len(parts),
        out_specs=VMEM,
        scratch_shapes=[pltpu.VMEM((1024, 128), F32)],
        compiler_params=params(8),
        cost_estimate=cost(0, 6),
        name="finish",
    )(core, *parts)


AXES = ("ka", "aux")


def moved(x, points, parts, source):
    route = []
    for k in range(points):
        for a in range(parts):
            k2, a2 = source(k, a)
            route.append((k2 * parts + a2, k * parts + a))
    return lax.ppermute(x, AXES, route)


def pass_kernel(x, done, out):
    pass


def after(x, done):
    return pl.pallas_call(
        pass_kernel,
        out_shape=jax.ShapeDtypeStruct(x.shape, x.dtype),
        in_specs=[ANY] * 2,
        out_specs=ANY,
        input_output_aliases={0: 0},
        compiler_params=params(1),
        cost_estimate=cost(0, 0),
        name="after",
    )(x, done)


def body(lambda_blocks, left_tiles, right_tiles):
    points, parts = lax.axis_size("ka"), lax.axis_size("aux")
    go = lambda x, source: moved(x, points, parts, source)
    near = lambda x: go(x, lambda k, a: ((k + 1) % points, a))
    far = lambda x: go(x, lambda k, a: ((k + points // 4) % points, a))
    zed = lambda x: go(x, lambda k, a: (k, a ^ 2))
    core = lambda x: go(x, lambda k, a: (k, a ^ 1))
    which = (lax.axis_index("aux") % 2).astype(jnp.int32).reshape(1)

    lam, again = flat_lambda(lambda_blocks.reshape(32, 64, 64))
    lam_z, far_own = zed(lam), far(lam)
    factors, done = {}, lam
    for s in (1, 0):
        done, sent = flat_factors(which, left_tiles[0], right_tiles[0], s, done)
        factors[s] = done, sent, core(sent)
    w_far = [build(0, *factors[1], done)]
    near_own = near(after(again, w_far[0]))
    w_far.append(build(HALF, *factors[1], w_far[0], 40000))
    lam_z, near_own, far_own = [after(x, w_far[1]) for x in (lam_z, near_own, far_own)]
    far_z, near_z = far(lam_z), near(lam_z)
    w_near = [build(0, *factors[0], near_own)]
    w_near.append(build(HALF, *factors[0], w_near[0]))
    far_z, near_z = after(far_z, w_near[1]), after(near_z, w_near[1])
    so_far = contract([far_own, core(far_own), far_z, core(far_z)], w_far)
    pieces = [near_own, core(near_own), near_z, core(near_z)]
    p_own, p_core, p_zed, p_diag = contract(pieces, w_near, so_far[0])
    out = finish(which, [p_own, zed(p_zed), core(p_core), zed(core(p_diag))])
    return out.reshape(lambda_blocks.shape)


def solution(mesh):
    placed = P("ka", None, "aux", None, None)
    return jax.shard_map(body, mesh=mesh, in_specs=(placed,) * 3, out_specs=placed, check_vma=False)
```

profile of v0, /device:TPU:96, one launch (start us, length us, event | category | flops | bytes accessed | tf_op | source)
XLA Modules:
  0.0 66.6 jit_solution(4754156961393145340)
XLA Ops:
  0.0 1.6 %flat_lambda.1 = (bf16[32,4096]{1,0:T(8,128)(2,1)S(1)}, bf16[32,4096]{1,0:T(8,128)(2,1)S(1)}) custom-call(bf16[32,64,64]{2,1,0:T(8,128)(2,1)} %bitcast.9), custom_call_target="tpu_custom_call" | custom-call | bytes 6144 | tf_op jit(solution)/shard_map/flat_lambda/pallas_call | solution.py:59
  1.6 3.1 %flat_factors.2 = (bf16[64,2048]{1,0:T(8,128)(2,1)S(1)}, bf16[64,6144]{1,0:T(8,128)(2,1)S(1)}) custom-call(s32[1]{0:T(128)} %bitcast.core, bf16[2,64,64,64]{3,2,1,0:T(8,128)(2,1)} %bitcast.5, bf16[2,64,64,64]{3,2,1,0:T(8,128)(2,1)} %bitcast.7, bf16[32,4096]{1,0:T(8,128)(2,1)S(1)} %get-tuple-element.16.done), custom_call_target="tpu_custom_call" | custom-call | bytes 409600000 | tf_op jit(solution)/shard_map/flat_factors/pallas_call | solution.py:80
  4.9 4.6 %collective-permute-start.3 = (bf16[32,4096]{1,0:T(8,128)(2,1)S(1)}, bf16[32,4096]{1,0:T(8,128)(2,1)S(1)}, u32[]{:S(2)}, u32[]{:S(2)}) collective-permute-start(bf16[32,4096]{1,0:T(8,128)(2,1)S(1)} %get-tuple-element.16.done), channel_id=1, source_target_pairs={{2,0},{3,1},{0,2},{1,3},{6,4},{7,5},{4,6},{5,7},{10,8},{11,9},{8,1... | collective-permute-start | bytes 786440 | tf_op jit(solution)/shard_map/ppermute | solution.py:234
  9.4 2.8 %collective-permute-start.7 = (bf16[32,4096]{1,0:T(8,128)(2,1)S(1)}, bf16[32,4096]{1,0:T(8,128)(2,1)S(1)}, u32[]{:S(2)}, u32[]{:S(2)}) collective-permute-start(bf16[32,4096]{1,0:T(8,128)(2,1)S(1)} %get-tuple-element.16.done), channel_id=1, source_target_pairs={{64,0},{65,1},{66,2},{67,3},{68,4},{69,5},{70,6},{71,7},{72,8},{73... | collective-permute-start | bytes 786440 | tf_op jit(solution)/shard_map/ppermute | solution.py:234
  12.2 3.1 %flat_factors.3 = (bf16[64,2048]{1,0:T(8,128)(2,1)S(1)}, bf16[64,6144]{1,0:T(8,128)(2,1)S(1)}) custom-call(s32[1]{0:T(128)} %bitcast.core, bf16[2,64,64,64]{3,2,1,0:T(8,128)(2,1)} %bitcast.6, bf16[2,64,64,64]{3,2,1,0:T(8,128)(2,1)} %bitcast.8, bf16[64,2048]{1,0:T(8,128)(2,1)S(1)} %get-tuple-element.17.done.mine), custom_call_target="tpu_custom_call" | custom-call | bytes 409600000 | tf_op jit(solution)/shard_map/flat_factors/pallas_call | solution.py:80
  15.4 3.8 %build_w.4.done.refs_4_ = bf16[2048,2048]{1,0:T(8,128)(2,1)S(1)} custom-call(bf16[64,2048]{1,0:T(8,128)(2,1)S(1)} %get-tuple-element.17.done.mine, bf16[64,6144]{1,0:T(8,128)(2,1)S(1)} %get-tuple-element.18.sent, bf16[64,6144]{1,0:T(8,128)(2,1)S(1)} %collective-permute-done.got_here, bf16[64,2048]{1,0:T(8,128)(2,1)S(1)} %get-tuple-element.19.done.mine), custom_call_target="tpu_custom_call" | custom-call | flops 2147483 | bytes 9216 | tf_op jit(solution)/shard_map/build_w/pallas_call | solution.py:138
  19.3 3.5 %collective-permute-start.1 = (bf16[32,4096]{1,0:T(8,128)(2,1)S(1)}, bf16[32,4096]{1,0:T(8,128)(2,1)S(1)}, u32[]{:S(2)}, u32[]{:S(2)}) collective-permute-start(bf16[32,4096]{1,0:T(8,128)(2,1)S(1)} %after.6), channel_id=1, source_target_pairs={{4,0},{5,1},{6,2},{7,3},{8,4},{9,5},{10,6},{11,7},{12,8},{13,9},{1... | collective-permute-start | bytes 786440 | tf_op jit(solution)/shard_map/ppermute | solution.py:234
  22.8 3.8 %build_w.5.done.refs_5_ = bf16[2048,2048]{1,0:T(8,128)(2,1)S(1)} custom-call(bf16[64,2048]{1,0:T(8,128)(2,1)S(1)} %get-tuple-element.17.done.mine, bf16[64,6144]{1,0:T(8,128)(2,1)S(1)} %get-tuple-element.18.sent, bf16[64,6144]{1,0:T(8,128)(2,1)S(1)} %collective-permute-done.got_here, bf16[2048,2048]{1,0:T(8,128)(2,1)S(1)} %build_w.4.done.refs_4_), custom_call_target="tpu_custom_call" | custom-call | flops 85899345920 | bytes 368640000 | tf_op jit(solution)/shard_map/build_w/pallas_call | solution.py:138
  26.6 0.9 %collective-permute-start.9 = (bf16[32,4096]{1,0:T(8,128)(2,1)S(1)}, bf16[32,4096]{1,0:T(8,128)(2,1)S(1)}, u32[]{:S(2)}, u32[]{:S(2)}) collective-permute-start(bf16[32,4096]{1,0:T(8,128)(2,1)S(1)} %after.8), channel_id=1, source_target_pairs={{64,0},{65,1},{66,2},{67,3},{68,4},{69,5},{70,6},{71,7},{72,8},{73... | collective-permute-start | bytes 786440 | tf_op jit(solution)/shard_map/ppermute | solution.py:234
  27.5 1.1 %collective-permute-start.4 = (bf16[32,4096]{1,0:T(8,128)(2,1)S(1)}, bf16[32,4096]{1,0:T(8,128)(2,1)S(1)}, u32[]{:S(2)}, u32[]{:S(2)}) collective-permute-start(bf16[32,4096]{1,0:T(8,128)(2,1)S(1)} %after.8), channel_id=1, source_target_pairs={{4,0},{5,1},{6,2},{7,3},{8,4},{9,5},{10,6},{11,7},{12,8},{13,9},{1... | collective-permute-start | bytes 786440 | tf_op jit(solution)/shard_map/ppermute | solution.py:234
  28.6 0.8 %collective-permute-done.1.x = bf16[32,4096]{1,0:T(8,128)(2,1)S(1)} collective-permute-done((bf16[32,4096]{1,0:T(8,128)(2,1)S(1)}, bf16[32,4096]{1,0:T(8,128)(2,1)S(1)}, u32[]{:S(2)}, u32[]{:S(2)}) %collective-permute-start.1) | collective-permute-done | bytes 262176 | tf_op jit(solution)/shard_map/ppermute | solution.py:234
  29.4 3.8 %build_w.6.done.refs_4_ = bf16[2048,2048]{1,0:T(8,128)(2,1)S(1)} custom-call(bf16[64,2048]{1,0:T(8,128)(2,1)S(1)} %get-tuple-element.19.done.mine, bf16[64,6144]{1,0:T(8,128)(2,1)S(1)} %get-tuple-element.20.sent, bf16[64,6144]{1,0:T(8,128)(2,1)S(1)} %collective-permute-done.5.got_here, bf16[32,4096]{1,0:T(8,128)(2,1)S(1)} %after.7.done.refs_0_), custom_call_target="tpu_custom_call" | custom-call | flops 2147483 | bytes 9216 | tf_op jit(solution)/shard_map/build_w/pallas_call | solution.py:138
  33.2 3.8 %build_w.7.done.refs_5_ = bf16[2048,2048]{1,0:T(8,128)(2,1)S(1)} custom-call(bf16[64,2048]{1,0:T(8,128)(2,1)S(1)} %get-tuple-element.19.done.mine, bf16[64,6144]{1,0:T(8,128)(2,1)S(1)} %get-tuple-element.20.sent, bf16[64,6144]{1,0:T(8,128)(2,1)S(1)} %collective-permute-done.5.got_here, bf16[2048,2048]{1,0:T(8,128)(2,1)S(1)} %build_w.6.done.refs_4_), custom_call_target="tpu_custom_call" | custom-call | flops 2147483 | bytes 9216 | tf_op jit(solution)/shard_map/build_w/pallas_call | solution.py:138
  37.0 7.4 %collective-permute-done.9.x = bf16[32,4096]{1,0:T(8,128)(2,1)S(1)} collective-permute-done((bf16[32,4096]{1,0:T(8,128)(2,1)S(1)}, bf16[32,4096]{1,0:T(8,128)(2,1)S(1)}, u32[]{:S(2)}, u32[]{:S(2)}) %collective-permute-start.9) | collective-permute-done | bytes 262176 | tf_op jit(solution)/shard_map/ppermute | solution.py:234
  44.5 0.5 collective-permute-start.6
  45.0 0.9 %collective-permute-done.10.refs_3_ = bf16[32,4096]{1,0:T(8,128)(2,1)S(1)} collective-permute-done((bf16[32,4096]{1,0:T(8,128)(2,1)S(1)}, bf16[32,4096]{1,0:T(8,128)(2,1)S(1)}, u32[]{:S(2)}, u32[]{:S(2)}) %collective-permute-start.10) | collective-permute-done | bytes 262176 | tf_op jit(solution)/shard_map/ppermute | solution.py:234
  45.9 2.5 %contract.2.refs_6_ = f32[128,2048]{1,0:T(8,128)S(1)} custom-call(bf16[32,4096]{1,0:T(8,128)(2,1)S(1)} %after.10.refs_0_, bf16[32,4096]{1,0:T(8,128)(2,1)S(1)} %collective-permute-done.8.refs_1_, bf16[32,4096]{1,0:T(8,128)(2,1)S(1)} %after.11.refs_2_, bf16[32,4096]{1,0:T(8,128)(2,1)S(1)} %collective-permute-done.10.refs_3_, ...), custom_call_target="tpu_custom_call" | custom-call | flops 2147483 | bytes 12288 | tf_op jit(solution)/shard_map/contract/pallas_call | solution.py:181
  48.4 2.5 %contract.3 = (f32[32,2048]{1,0:T(8,128)S(1)}, f32[32,2048]{1,0:T(8,128)S(1)}, bf16[32,2048]{1,0:T(8,128)(2,1)S(1)}, bf16[32,2048]{1,0:T(8,128)(2,1)S(1)}) custom-call(bf16[32,4096]{1,0:T(8,128)(2,1)S(1)} %after.7.done.refs_0_, bf16[32,4096]{1,0:T(8,128)(2,1)S(1)} %collective-permute-done.2.refs_1_, bf16[32,4096]{1,0:T(8,128)(2,1)S(1)} %after.9.refs_2_, ...), custom_call_target="tpu_custom_call" | custom-call | flops 2147483 | bytes 12288 | tf_op jit(solution)/shard_map/contract/pallas_call | solution.py:181
  51.1 0.4 collective-permute-start.12
  51.5 1.4 %collective-permute-start.11 = (bf16[32,2048]{1,0:T(8,128)(2,1)S(1)}, bf16[32,2048]{1,0:T(8,128)(2,1)S(1)}, u32[]{:S(2)}, u32[]{:S(2)}) collective-permute-start(bf16[32,2048]{1,0:T(8,128)(2,1)S(1)} %get-tuple-element.22), channel_id=1, source_target_pairs={{2,0},{3,1},{0,2},{1,3},{6,4},{7,5},{4,6},{5,7},{10,8},{11,9},{8,1... | collective-permute-start | bytes 393224 | tf_op jit(solution)/shard_map/ppermute | solution.py:234
  53.0 4.5 %collective-permute-start.14 = (bf16[32,2048]{1,0:T(8,128)(2,1)S(1)}, bf16[32,2048]{1,0:T(8,128)(2,1)S(1)}, u32[]{:S(2)}, u32[]{:S(2)}) collective-permute-start(bf16[32,2048]{1,0:T(8,128)(2,1)S(1)} %collective-permute-done.13), channel_id=1, source_target_pairs={{2,0},{3,1},{0,2},{1,3},{6,4},{7,5},{4,6},{5,7},{10,8},{11,9},{8,1... | collective-permute-start | bytes 393224 | tf_op jit(solution)/shard_map/ppermute | solution.py:234
  57.4 4.6 %collective-permute-done.11.refs_1_ = bf16[32,2048]{1,0:T(8,128)(2,1)S(1)} collective-permute-done((bf16[32,2048]{1,0:T(8,128)(2,1)S(1)}, bf16[32,2048]{1,0:T(8,128)(2,1)S(1)}, u32[]{:S(2)}, u32[]{:S(2)}) %collective-permute-start.11) | collective-permute-done | bytes 131104 | tf_op jit(solution)/shard_map/ppermute | solution.py:234
  62.1 2.7 %collective-permute-done.14.refs_3_ = bf16[32,2048]{1,0:T(8,128)(2,1)S(1)} collective-permute-done((bf16[32,2048]{1,0:T(8,128)(2,1)S(1)}, bf16[32,2048]{1,0:T(8,128)(2,1)S(1)}, u32[]{:S(2)}, u32[]{:S(2)}) %collective-permute-start.14) | collective-permute-done | bytes 131104 | tf_op jit(solution)/shard_map/ppermute | solution.py:234
  64.8 1.8 %finish.1 = f32[32,64,64]{2,1,0:T(8,128)} custom-call(s32[1]{0:T(128)} %bitcast.core, f32[32,2048]{1,0:T(8,128)S(1)} %get-tuple-element.21.refs_0_, bf16[32,2048]{1,0:T(8,128)(2,1)S(1)} %collective-permute-done.11.refs_1_, f32[32,2048]{1,0:T(8,128)S(1)} %collective-permute-done.12.refs_2_, bf16[32,2048]{1,0:T(8,128)(2,1)S(1)} %collective-permute-done.14.refs_3_), custom_call_target="tpu_custom_call" | custom-call | bytes 6144 | tf_op jit(solution)/shard_map/finish/pallas_call | solution.py:213
  (22 shorter events, 0.6 us)
Async XLA Ops:
  4.8 10.6 %collective-permute-start = (bf16[64,6144]{1,0:T(8,128)(2,1)S(1)}, bf16[64,6144]{1,0:T(8,128)(2,1)S(1)}, u32[]{:S(2)}, u32[]{:S(2)}) collective-permute-start(bf16[64,6144]{1,0:T(8,128)(2,1)S(1)} %get-tuple-element.18.sent), channel_id=1, source_target_pairs={{1,0},{0,1},{3,2},{2,3},{5,4},{4,5},{7,6},{6,7},{9,8},{8,9},{11,10... | collective-permute-start | bytes 2359304 | tf_op jit(solution)/shard_map/ppermute | solution.py:234
  4.9 21.7 %collective-permute-start.3 = (bf16[32,4096]{1,0:T(8,128)(2,1)S(1)}, bf16[32,4096]{1,0:T(8,128)(2,1)S(1)}, u32[]{:S(2)}, u32[]{:S(2)}) collective-permute-start(bf16[32,4096]{1,0:T(8,128)(2,1)S(1)} %get-tuple-element.16.done), channel_id=1, source_target_pairs={{2,0},{3,1},{0,2},{1,3},{6,4},{7,5},{4,6},{5,7},{10,8},{11,9},{8,1... | collective-permute-start | bytes 786440 | tf_op jit(solution)/shard_map/ppermute | solution.py:234
  9.4 19.2 %collective-permute-start.7 = (bf16[32,4096]{1,0:T(8,128)(2,1)S(1)}, bf16[32,4096]{1,0:T(8,128)(2,1)S(1)}, u32[]{:S(2)}, u32[]{:S(2)}) collective-permute-start(bf16[32,4096]{1,0:T(8,128)(2,1)S(1)} %get-tuple-element.16.done), channel_id=1, source_target_pairs={{64,0},{65,1},{66,2},{67,3},{68,4},{69,5},{70,6},{71,7},{72,8},{73... | collective-permute-start | bytes 786440 | tf_op jit(solution)/shard_map/ppermute | solution.py:234
  15.3 14.1 %collective-permute-start.5 = (bf16[64,6144]{1,0:T(8,128)(2,1)S(1)}, bf16[64,6144]{1,0:T(8,128)(2,1)S(1)}, u32[]{:S(2)}, u32[]{:S(2)}) collective-permute-start(bf16[64,6144]{1,0:T(8,128)(2,1)S(1)} %get-tuple-element.20.sent), channel_id=1, source_target_pairs={{1,0},{0,1},{3,2},{2,3},{5,4},{4,5},{7,6},{6,7},{9,8},{8,9},{11,10... | collective-permute-start | bytes 2359304 | tf_op jit(solution)/shard_map/ppermute | solution.py:234
  19.3 10.1 %collective-permute-start.1 = (bf16[32,4096]{1,0:T(8,128)(2,1)S(1)}, bf16[32,4096]{1,0:T(8,128)(2,1)S(1)}, u32[]{:S(2)}, u32[]{:S(2)}) collective-permute-start(bf16[32,4096]{1,0:T(8,128)(2,1)S(1)} %after.6), channel_id=1, source_target_pairs={{4,0},{5,1},{6,2},{7,3},{8,4},{9,5},{10,6},{11,7},{12,8},{13,9},{1... | collective-permute-start | bytes 786440 | tf_op jit(solution)/shard_map/ppermute | solution.py:234
  26.6 17.8 %collective-permute-start.9 = (bf16[32,4096]{1,0:T(8,128)(2,1)S(1)}, bf16[32,4096]{1,0:T(8,128)(2,1)S(1)}, u32[]{:S(2)}, u32[]{:S(2)}) collective-permute-start(bf16[32,4096]{1,0:T(8,128)(2,1)S(1)} %after.8), channel_id=1, source_target_pairs={{64,0},{65,1},{66,2},{67,3},{68,4},{69,5},{70,6},{71,7},{72,8},{73... | collective-permute-start | bytes 786440 | tf_op jit(solution)/shard_map/ppermute | solution.py:234
  27.5 16.9 %collective-permute-start.4 = (bf16[32,4096]{1,0:T(8,128)(2,1)S(1)}, bf16[32,4096]{1,0:T(8,128)(2,1)S(1)}, u32[]{:S(2)}, u32[]{:S(2)}) collective-permute-start(bf16[32,4096]{1,0:T(8,128)(2,1)S(1)} %after.8), channel_id=1, source_target_pairs={{4,0},{5,1},{6,2},{7,3},{8,4},{9,5},{10,6},{11,7},{12,8},{13,9},{1... | collective-permute-start | bytes 786440 | tf_op jit(solution)/shard_map/ppermute | solution.py:234
  28.6 16.4 %collective-permute-start.8 = (bf16[32,4096]{1,0:T(8,128)(2,1)S(1)}, bf16[32,4096]{1,0:T(8,128)(2,1)S(1)}, u32[]{:S(2)}, u32[]{:S(2)}) collective-permute-start(bf16[32,4096]{1,0:T(8,128)(2,1)S(1)} %after.10.refs_0_), channel_id=1, source_target_pairs={{1,0},{0,1},{3,2},{2,3},{5,4},{4,5},{7,6},{6,7},{9,8},{8,9},{11,10... | collective-permute-start | bytes 786440 | tf_op jit(solution)/shard_map/ppermute | solution.py:234
  44.4 1.5 %collective-permute-start.10 = (bf16[32,4096]{1,0:T(8,128)(2,1)S(1)}, bf16[32,4096]{1,0:T(8,128)(2,1)S(1)}, u32[]{:S(2)}, u32[]{:S(2)}) collective-permute-start(bf16[32,4096]{1,0:T(8,128)(2,1)S(1)} %after.11.refs_2_), channel_id=1, source_target_pairs={{1,0},{0,1},{3,2},{2,3},{5,4},{4,5},{7,6},{6,7},{9,8},{8,9},{11,10... | collective-permute-start | bytes 786440 | tf_op jit(solution)/shard_map/ppermute | solution.py:234
  44.5 4.0 %collective-permute-start.6 = (bf16[32,4096]{1,0:T(8,128)(2,1)S(1)}, bf16[32,4096]{1,0:T(8,128)(2,1)S(1)}, u32[]{:S(2)}, u32[]{:S(2)}) collective-permute-start(bf16[32,4096]{1,0:T(8,128)(2,1)S(1)} %after.9.refs_2_), channel_id=1, source_target_pairs={{1,0},{0,1},{3,2},{2,3},{5,4},{4,5},{7,6},{6,7},{9,8},{8,9},{11,10... | collective-permute-start | bytes 786440 | tf_op jit(solution)/shard_map/ppermute | solution.py:234
  44.9 3.5 %collective-permute-start.2 = (bf16[32,4096]{1,0:T(8,128)(2,1)S(1)}, bf16[32,4096]{1,0:T(8,128)(2,1)S(1)}, u32[]{:S(2)}, u32[]{:S(2)}) collective-permute-start(bf16[32,4096]{1,0:T(8,128)(2,1)S(1)} %after.7.done.refs_0_), channel_id=1, source_target_pairs={{1,0},{0,1},{3,2},{2,3},{5,4},{4,5},{7,6},{6,7},{9,8},{8,9},{11,10... | collective-permute-start | bytes 786440 | tf_op jit(solution)/shard_map/ppermute | solution.py:234
  50.9 2.0 %collective-permute-start.13 = (bf16[32,2048]{1,0:T(8,128)(2,1)S(1)}, bf16[32,2048]{1,0:T(8,128)(2,1)S(1)}, u32[]{:S(2)}, u32[]{:S(2)}) collective-permute-start(bf16[32,2048]{1,0:T(8,128)(2,1)S(1)} %get-tuple-element.24), channel_id=1, source_target_pairs={{1,0},{0,1},{3,2},{2,3},{5,4},{4,5},{7,6},{6,7},{9,8},{8,9},{11,10... | collective-permute-start | bytes 393224 | tf_op jit(solution)/shard_map/ppermute | solution.py:234
  51.1 13.7 %collective-permute-start.12 = (f32[32,2048]{1,0:T(8,128)S(1)}, f32[32,2048]{1,0:T(8,128)S(1)}, u32[]{:S(2)}, u32[]{:S(2)}) collective-permute-start(f32[32,2048]{1,0:T(8,128)S(1)} %get-tuple-element.23), channel_id=1, source_target_pairs={{1,0},{0,1},{3,2},{2,3},{5,4},{4,5},{7,6},{6,7},{9,8},{8,9},{11,10... | collective-permute-start | bytes 786440 | tf_op jit(solution)/shard_map/ppermute | solution.py:234
  51.5 10.6 %collective-permute-start.11 = (bf16[32,2048]{1,0:T(8,128)(2,1)S(1)}, bf16[32,2048]{1,0:T(8,128)(2,1)S(1)}, u32[]{:S(2)}, u32[]{:S(2)}) collective-permute-start(bf16[32,2048]{1,0:T(8,128)(2,1)S(1)} %get-tuple-element.22), channel_id=1, source_target_pairs={{2,0},{3,1},{0,2},{1,3},{6,4},{7,5},{4,6},{5,7},{10,8},{11,9},{8,1... | collective-permute-start | bytes 393224 | tf_op jit(solution)/shard_map/ppermute | solution.py:234
  53.0 11.9 %collective-permute-start.14 = (bf16[32,2048]{1,0:T(8,128)(2,1)S(1)}, bf16[32,2048]{1,0:T(8,128)(2,1)S(1)}, u32[]{:S(2)}, u32[]{:S(2)}) collective-permute-start(bf16[32,2048]{1,0:T(8,128)(2,1)S(1)} %collective-permute-done.13), channel_id=1, source_target_pairs={{2,0},{3,1},{0,2},{1,3},{6,4},{7,5},{4,6},{5,7},{10,8},{11,9},{8,1... | collective-permute-start | bytes 393224 | tf_op jit(solution)/shard_map/ppermute | solution.py:234
where the time goes:
time: 67.9 us; the launch traced here: 66.6 us
  Pallas kernels  29.8 us (44%)
  starting transfers between devices  20.2 us (30%)
  waiting for transfers between devices  16.5 us (24%)
    ppermute x15, starting transfers between devices, moved(): return lax.ppermute(x, AXES, route)  20.2 us
    ppermute x15, waiting for transfers between devices, moved(): return lax.ppermute(x, AXES, route)  16.5 us
    pallas_call x4, Pallas kernels, build(): pl.pallas_call(functools.partial(build_kernel, first), out_shape=pltpu.VM...  15.3 us
    pallas_call x2, Pallas kernels, flat_factors(): pl.pallas_call(factor_kernel, grid=(2,), out_shape=[jax.ShapeDtypeStruct(...  6.19 us
    pallas_call x2, Pallas kernels, contract(): pl.pallas_call(functools.partial(contract_kernel, last, first), out_shape...  4.93 us
    pallas_call x1, Pallas kernels, finish(): pl.pallas_call(finish_kernel, out_shape=jax.ShapeDtypeStruct((32, 64, 64)...  1.76 us
    pallas_call x1, Pallas kernels, flat_lambda(): pl.pallas_call(lambda_kernel, grid=(1,), out_shape=[jax.ShapeDtypeStruct(...  1.63 us
  transfers between devices with their start and end apart: 15, of which 5 were waited for; matrix products, arithmetic and copies ran while one was open for 0% of the time, Pallas kernels for 31%

commit v1 on v0

--- a/solution.py
+++ b/solution.py
@@ -90,7 +90,7 @@
     )(core, in_hbm(left), in_hbm(right), done)
 
 
-TS = 4
+TS = 8
 HALF = 16
 
 
@@ -104,8 +104,8 @@
 
     def fill(slot, u):
         for i in range(TS):
-            t = first + jnp.minimum(u * TS + i, HALF - 1)
-            at = pl.ds(pl.multiple_of(2048 + t * 128, 128), 128)
+            t = first + u * TS + i
+            at = slice(2048 + t * 128, 2048 + (t + 1) * 128)
             v = jnp.concatenate([sent[:, at], got_here[:, at]], axis=0)
             r = jnp.concatenate([v[:, 64:], v[:, :64]], axis=1)
             a, b = i * 256, i * 256 + 128
@@ -115,23 +115,25 @@
             s[slot, 128:256, b : b + 128] = jnp.where(low, zero, v)
 
     def work(u, slot):
-        fill(1 - slot, u + 1)
-        for m in range(8):
-            got = jnp.dot(x[m * 128 : (m + 1) * 128, :], s[slot], preferred_element_type=F32).astype(BF16)
-            for i in range(TS * 2):
-                at = pl.ds(pl.multiple_of((u * TS * 2 + i) * 64, 64), 64)
-                for p in range(2):
-                    w[at, (m * 2 + p) * 128 : (m * 2 + p + 1) * 128] = got[
-                        p * 64 : (p + 1) * 64, i * 128 : (i + 1) * 128
-                    ]
-
-    def pair(v, _):
-        work(v * 2, 0)
-        work(v * 2 + 1, 1)
-        return 0
+        if u + 1 < HALF // TS:
+            fill(1 - slot, u + 1)
+        for n in range(TS // 2):
+            for m in range(8):
+                got = jnp.dot(
+                    x[m * 128 : (m + 1) * 128, :],
+                    s[slot, :, n * 512 : (n + 1) * 512],
+                    preferred_element_type=F32,
+                ).astype(BF16)
+                for i in range(4):
+                    row = (u * TS * 2 + n * 4 + i) * 64
+                    for p in range(2):
+                        w[row : row + 64, (m * 2 + p) * 128 : (m * 2 + p + 1) * 128] = got[
+                            p * 64 : (p + 1) * 64, i * 128 : (i + 1) * 128
+                        ]
 
     fill(0, 0)
-    lax.fori_loop(0, HALF // TS // 2, pair, 0)
+    for u in range(HALF // TS):
+        work(u, u % 2)
 
 
 def build(first, mine, sent, got, done, weight=1):
@@ -269,10 +271,11 @@
     w_far = [build(0, *factors[1], done)]
     near_own = near(after(again, w_far[0]))
     w_far.append(build(HALF, *factors[1], w_far[0], 40000))
-    lam_z, near_own, far_own = [after(x, w_far[1]) for x in (lam_z, near_own, far_own)]
+    lam_z, far_own = after(lam_z, w_far[1]), after(far_own, w_far[1])
     far_z, near_z = far(lam_z), near(lam_z)
-    w_near = [build(0, *factors[0], near_own)]
-    w_near.append(build(HALF, *factors[0], w_near[0]))
+    w_near = [build(0, *factors[0], lam_z)]
+    near_own = after(near_own, w_near[0])
+    w_near.append(build(HALF, *factors[0], near_own))
     far_z, near_z = after(far_z, w_near[1]), after(near_z, w_near[1])
     so_far = contract([far_own, core(far_own), far_z, core(far_z)], w_far)
     pieces = [near_own, core(near_own), near_z, core(near_z)]

time: 67.9 us -> 64.9 us (0.956); the launches traced: 66.6 us -> 64.7 us
  Pallas kernels: 29.8 us -> 26 us
  starting transfers between devices: 20.2 us -> 22.2 us
    pallas_call x4, Pallas kernels: 15.3 us -> 11.5 us  [build(): pl.pallas_call(functools.partial(build_kernel, first), out_shape=pltpu.VM...]
    ppermute x15, starting transfers between devices: 20.2 us -> 22.2 us  [moved(): return lax.ppermute(x, AXES, route)]
  transfers between devices with their start and end apart: 15 -> 15, of which waited for: 5 -> 4; matrix products, arithmetic and copies ran while one was open for 0% -> 0% of each run, Pallas kernels for 31% -> 26%
where the time goes in v1:
time: 64.9 us; the launch traced here: 64.7 us
  Pallas kernels  26 us (40%)
  starting transfers between devices  22.2 us (34%)
  waiting for transfers between devices  16.3 us (25%)
    ppermute x15, starting transfers between devices, moved(): return lax.ppermute(x, AXES, route)  22.2 us
    ppermute x15, waiting for transfers between devices, moved(): return lax.ppermute(x, AXES, route)  16.3 us
    pallas_call x4, Pallas kernels, build(): pl.pallas_call(functools.partial(build_kernel, first), out_shape=pltpu.VM...  11.5 us
    pallas_call x2, Pallas kernels, flat_factors(): pl.pallas_call(factor_kernel, grid=(2,), out_shape=[jax.ShapeDtypeStruct(...  6.19 us
    pallas_call x2, Pallas kernels, contract(): pl.pallas_call(functools.partial(contract_kernel, last, first), out_shape...  4.93 us
    pallas_call x1, Pallas kernels, finish(): pl.pallas_call(finish_kernel, out_shape=jax.ShapeDtypeStruct((32, 64, 64)...  1.76 us
    pallas_call x1, Pallas kernels, flat_lambda(): pl.pallas_call(lambda_kernel, grid=(1,), out_shape=[jax.ShapeDtypeStruct(...  1.63 us
  transfers between devices with their start and end apart: 15, of which 4 were waited for; matrix products, arithmetic and copies ran while one was open for 0% of the time, Pallas kernels for 26%

profile of v1, /device:TPU:96, one launch (start us, length us, event | category | flops | bytes accessed | tf_op | source)
XLA Modules:
  0.0 64.7 jit_solution(10318757597682422503)
XLA Ops:
  0.0 1.6 %flat_lambda.1 = (bf16[32,4096]{1,0:T(8,128)(2,1)S(1)}, bf16[32,4096]{1,0:T(8,128)(2,1)S(1)}) custom-call(bf16[32,64,64]{2,1,0:T(8,128)(2,1)} %bitcast.9), custom_call_target="tpu_custom_call" | custom-call | bytes 6144 | tf_op jit(solution)/shard_map/flat_lambda/pallas_call | solution.py:59
  1.6 3.1 %flat_factors.2 = (bf16[64,2048]{1,0:T(8,128)(2,1)S(1)}, bf16[64,6144]{1,0:T(8,128)(2,1)S(1)}) custom-call(s32[1]{0:T(128)} %bitcast.core, bf16[2,64,64,64]{3,2,1,0:T(8,128)(2,1)} %bitcast.5, bf16[2,64,64,64]{3,2,1,0:T(8,128)(2,1)} %bitcast.7, bf16[32,4096]{1,0:T(8,128)(2,1)S(1)} %get-tuple-element.16.done), custom_call_target="tpu_custom_call" | custom-call | bytes 409600000 | tf_op jit(solution)/shard_map/flat_factors/pallas_call | solution.py:80
  4.9 4.6 %collective-permute-start.3 = (bf16[32,4096]{1,0:T(8,128)(2,1)S(1)}, bf16[32,4096]{1,0:T(8,128)(2,1)S(1)}, u32[]{:S(2)}, u32[]{:S(2)}) collective-permute-start(bf16[32,4096]{1,0:T(8,128)(2,1)S(1)} %get-tuple-element.16.done), channel_id=1, source_target_pairs={{2,0},{3,1},{0,2},{1,3},{6,4},{7,5},{4,6},{5,7},{10,8},{11,9},{8,1... | collective-permute-start | bytes 786440 | tf_op jit(solution)/shard_map/ppermute | solution.py:236
  9.4 2.8 %collective-permute-start.7 = (bf16[32,4096]{1,0:T(8,128)(2,1)S(1)}, bf16[32,4096]{1,0:T(8,128)(2,1)S(1)}, u32[]{:S(2)}, u32[]{:S(2)}) collective-permute-start(bf16[32,4096]{1,0:T(8,128)(2,1)S(1)} %get-tuple-element.16.done), channel_id=1, source_target_pairs={{64,0},{65,1},{66,2},{67,3},{68,4},{69,5},{70,6},{71,7},{72,8},{73... | collective-permute-start | bytes 786440 | tf_op jit(solution)/shard_map/ppermute | solution.py:236
  12.2 3.1 %flat_factors.3 = (bf16[64,2048]{1,0:T(8,128)(2,1)S(1)}, bf16[64,6144]{1,0:T(8,128)(2,1)S(1)}) custom-call(s32[1]{0:T(128)} %bitcast.core, bf16[2,64,64,64]{3,2,1,0:T(8,128)(2,1)} %bitcast.6, bf16[2,64,64,64]{3,2,1,0:T(8,128)(2,1)} %bitcast.8, bf16[64,2048]{1,0:T(8,128)(2,1)S(1)} %get-tuple-element.17.done.mine), custom_call_target="tpu_custom_call" | custom-call | bytes 409600000 | tf_op jit(solution)/shard_map/flat_factors/pallas_call | solution.py:80
  15.4 2.9 %build_w.4.done.refs_4_ = bf16[2048,2048]{1,0:T(8,128)(2,1)S(1)} custom-call(bf16[64,2048]{1,0:T(8,128)(2,1)S(1)} %get-tuple-element.17.done.mine, bf16[64,6144]{1,0:T(8,128)(2,1)S(1)} %get-tuple-element.18.sent, bf16[64,6144]{1,0:T(8,128)(2,1)S(1)} %collective-permute-done.got_here, bf16[64,2048]{1,0:T(8,128)(2,1)S(1)} %get-tuple-element.19.done.mine), custom_call_target="tpu_custom_call" | custom-call | flops 2147483 | bytes 9216 | tf_op jit(solution)/shard_map/build_w/pallas_call | solution.py:140
  18.3 3.5 %collective-permute-start.1 = (bf16[32,4096]{1,0:T(8,128)(2,1)S(1)}, bf16[32,4096]{1,0:T(8,128)(2,1)S(1)}, u32[]{:S(2)}, u32[]{:S(2)}) collective-permute-start(bf16[32,4096]{1,0:T(8,128)(2,1)S(1)} %after.6), channel_id=1, source_target_pairs={{4,0},{5,1},{6,2},{7,3},{8,4},{9,5},{10,6},{11,7},{12,8},{13,9},{1... | collective-permute-start | bytes 786440 | tf_op jit(solution)/shard_map/ppermute | solution.py:236
  21.8 2.9 %build_w.5.done.refs_5_ = bf16[2048,2048]{1,0:T(8,128)(2,1)S(1)} custom-call(bf16[64,2048]{1,0:T(8,128)(2,1)S(1)} %get-tuple-element.17.done.mine, bf16[64,6144]{1,0:T(8,128)(2,1)S(1)} %get-tuple-element.18.sent, bf16[64,6144]{1,0:T(8,128)(2,1)S(1)} %collective-permute-done.got_here, bf16[2048,2048]{1,0:T(8,128)(2,1)S(1)} %build_w.4.done.refs_4_), custom_call_target="tpu_custom_call" | custom-call | flops 85899345920 | bytes 368640000 | tf_op jit(solution)/shard_map/build_w/pallas_call | solution.py:140
  24.7 0.9 %collective-permute-start.9 = (bf16[32,4096]{1,0:T(8,128)(2,1)S(1)}, bf16[32,4096]{1,0:T(8,128)(2,1)S(1)}, u32[]{:S(2)}, u32[]{:S(2)}) collective-permute-start(bf16[32,4096]{1,0:T(8,128)(2,1)S(1)} %after.7.done), channel_id=1, source_target_pairs={{64,0},{65,1},{66,2},{67,3},{68,4},{69,5},{70,6},{71,7},{72,8},{73... | collective-permute-start | bytes 786440 | tf_op jit(solution)/shard_map/ppermute | solution.py:236
  25.6 3.0 %collective-permute-start.5 = (bf16[32,4096]{1,0:T(8,128)(2,1)S(1)}, bf16[32,4096]{1,0:T(8,128)(2,1)S(1)}, u32[]{:S(2)}, u32[]{:S(2)}) collective-permute-start(bf16[32,4096]{1,0:T(8,128)(2,1)S(1)} %after.7.done), channel_id=1, source_target_pairs={{4,0},{5,1},{6,2},{7,3},{8,4},{9,5},{10,6},{11,7},{12,8},{13,9},{1... | collective-permute-start | bytes 786440 | tf_op jit(solution)/shard_map/ppermute | solution.py:236
  28.6 2.9 %build_w.6.done.refs_4_ = bf16[2048,2048]{1,0:T(8,128)(2,1)S(1)} custom-call(bf16[64,2048]{1,0:T(8,128)(2,1)S(1)} %get-tuple-element.19.done.mine, bf16[64,6144]{1,0:T(8,128)(2,1)S(1)} %get-tuple-element.20.sent, bf16[64,6144]{1,0:T(8,128)(2,1)S(1)} %collective-permute-done.2.got_here, bf16[32,4096]{1,0:T(8,128)(2,1)S(1)} %after.7.done), custom_call_target="tpu_custom_call" | custom-call | flops 2147483 | bytes 9216 | tf_op jit(solution)/shard_map/build_w/pallas_call | solution.py:140
  31.5 2.9 %build_w.7.done.refs_5_ = bf16[2048,2048]{1,0:T(8,128)(2,1)S(1)} custom-call(bf16[64,2048]{1,0:T(8,128)(2,1)S(1)} %get-tuple-element.19.done.mine, bf16[64,6144]{1,0:T(8,128)(2,1)S(1)} %get-tuple-element.20.sent, bf16[64,6144]{1,0:T(8,128)(2,1)S(1)} %collective-permute-done.2.got_here, bf16[32,4096]{1,0:T(8,128)(2,1)S(1)} %after.8.done.refs_0_), custom_call_target="tpu_custom_call" | custom-call | flops 2147483 | bytes 9216 | tf_op jit(solution)/shard_map/build_w/pallas_call | solution.py:140
  34.4 9.0 %collective-permute-done.9.x = bf16[32,4096]{1,0:T(8,128)(2,1)S(1)} collective-permute-done((bf16[32,4096]{1,0:T(8,128)(2,1)S(1)}, bf16[32,4096]{1,0:T(8,128)(2,1)S(1)}, u32[]{:S(2)}, u32[]{:S(2)}) %collective-permute-start.9) | collective-permute-done | bytes 262176 | tf_op jit(solution)/shard_map/ppermute | solution.py:236
  43.5 0.5 collective-permute-start.6
  44.2 0.8 %collective-permute-done.10.refs_3_ = bf16[32,4096]{1,0:T(8,128)(2,1)S(1)} collective-permute-done((bf16[32,4096]{1,0:T(8,128)(2,1)S(1)}, bf16[32,4096]{1,0:T(8,128)(2,1)S(1)}, u32[]{:S(2)}, u32[]{:S(2)}) %collective-permute-start.10) | collective-permute-done | bytes 262176 | tf_op jit(solution)/shard_map/ppermute | solution.py:236
  45.0 2.5 %contract.2.refs_6_ = f32[128,2048]{1,0:T(8,128)S(1)} custom-call(bf16[32,4096]{1,0:T(8,128)(2,1)S(1)} %after.10.refs_0_, bf16[32,4096]{1,0:T(8,128)(2,1)S(1)} %collective-permute-done.8.refs_1_, bf16[32,4096]{1,0:T(8,128)(2,1)S(1)} %after.11.refs_2_, bf16[32,4096]{1,0:T(8,128)(2,1)S(1)} %collective-permute-done.10.refs_3_, ...), custom_call_target="tpu_custom_call" | custom-call | flops 2147483 | bytes 12288 | tf_op jit(solution)/shard_map/contract/pallas_call | solution.py:183
  47.5 2.5 %contract.3 = (f32[32,2048]{1,0:T(8,128)S(1)}, f32[32,2048]{1,0:T(8,128)S(1)}, bf16[32,2048]{1,0:T(8,128)(2,1)S(1)}, bf16[32,2048]{1,0:T(8,128)(2,1)S(1)}) custom-call(bf16[32,4096]{1,0:T(8,128)(2,1)S(1)} %after.8.done.refs_0_, bf16[32,4096]{1,0:T(8,128)(2,1)S(1)} %collective-permute-done.4.refs_1_, bf16[32,4096]{1,0:T(8,128)(2,1)S(1)} %after.9.refs_2_, ...), custom_call_target="tpu_custom_call" | custom-call | flops 2147483 | bytes 12288 | tf_op jit(solution)/shard_map/contract/pallas_call | solution.py:183
  50.0 0.2 collective-permute-start.13
  50.2 0.4 collective-permute-start.12
  50.6 1.5 %collective-permute-start.11 = (bf16[32,2048]{1,0:T(8,128)(2,1)S(1)}, bf16[32,2048]{1,0:T(8,128)(2,1)S(1)}, u32[]{:S(2)}, u32[]{:S(2)}) collective-permute-start(bf16[32,2048]{1,0:T(8,128)(2,1)S(1)} %get-tuple-element.22), channel_id=1, source_target_pairs={{2,0},{3,1},{0,2},{1,3},{6,4},{7,5},{4,6},{5,7},{10,8},{11,9},{8,1... | collective-permute-start | bytes 393224 | tf_op jit(solution)/shard_map/ppermute | solution.py:236
  52.1 4.4 %collective-permute-start.14 = (bf16[32,2048]{1,0:T(8,128)(2,1)S(1)}, bf16[32,2048]{1,0:T(8,128)(2,1)S(1)}, u32[]{:S(2)}, u32[]{:S(2)}) collective-permute-start(bf16[32,2048]{1,0:T(8,128)(2,1)S(1)} %collective-permute-done.13), channel_id=1, source_target_pairs={{2,0},{3,1},{0,2},{1,3},{6,4},{7,5},{4,6},{5,7},{10,8},{11,9},{8,1... | collective-permute-start | bytes 393224 | tf_op jit(solution)/shard_map/ppermute | solution.py:236
  56.5 4.3 %collective-permute-done.11.refs_1_ = bf16[32,2048]{1,0:T(8,128)(2,1)S(1)} collective-permute-done((bf16[32,2048]{1,0:T(8,128)(2,1)S(1)}, bf16[32,2048]{1,0:T(8,128)(2,1)S(1)}, u32[]{:S(2)}, u32[]{:S(2)}) %collective-permute-start.11) | collective-permute-done | bytes 131104 | tf_op jit(solution)/shard_map/ppermute | solution.py:236
  60.8 2.2 %collective-permute-done.14.refs_3_ = bf16[32,2048]{1,0:T(8,128)(2,1)S(1)} collective-permute-done((bf16[32,2048]{1,0:T(8,128)(2,1)S(1)}, bf16[32,2048]{1,0:T(8,128)(2,1)S(1)}, u32[]{:S(2)}, u32[]{:S(2)}) %collective-permute-start.14) | collective-permute-done | bytes 131104 | tf_op jit(solution)/shard_map/ppermute | solution.py:236
  63.0 1.8 %finish.1 = f32[32,64,64]{2,1,0:T(8,128)} custom-call(s32[1]{0:T(128)} %bitcast.core, f32[32,2048]{1,0:T(8,128)S(1)} %get-tuple-element.21.refs_0_, bf16[32,2048]{1,0:T(8,128)(2,1)S(1)} %collective-permute-done.11.refs_1_, f32[32,2048]{1,0:T(8,128)S(1)} %collective-permute-done.12.refs_2_, bf16[32,2048]{1,0:T(8,128)(2,1)S(1)} %collective-permute-done.14.refs_3_), custom_call_target="tpu_custom_call" | custom-call | bytes 6144 | tf_op jit(solution)/shard_map/finish/pallas_call | solution.py:215
  (22 shorter events, 0.5 us)
Async XLA Ops:
  4.8 10.6 %collective-permute-start = (bf16[64,6144]{1,0:T(8,128)(2,1)S(1)}, bf16[64,6144]{1,0:T(8,128)(2,1)S(1)}, u32[]{:S(2)}, u32[]{:S(2)}) collective-permute-start(bf16[64,6144]{1,0:T(8,128)(2,1)S(1)} %get-tuple-element.18.sent), channel_id=1, source_target_pairs={{1,0},{0,1},{3,2},{2,3},{5,4},{4,5},{7,6},{6,7},{9,8},{8,9},{11,10... | collective-permute-start | bytes 2359304 | tf_op jit(solution)/shard_map/ppermute | solution.py:236
  4.9 19.9 %collective-permute-start.3 = (bf16[32,4096]{1,0:T(8,128)(2,1)S(1)}, bf16[32,4096]{1,0:T(8,128)(2,1)S(1)}, u32[]{:S(2)}, u32[]{:S(2)}) collective-permute-start(bf16[32,4096]{1,0:T(8,128)(2,1)S(1)} %get-tuple-element.16.done), channel_id=1, source_target_pairs={{2,0},{3,1},{0,2},{1,3},{6,4},{7,5},{4,6},{5,7},{10,8},{11,9},{8,1... | collective-permute-start | bytes 786440 | tf_op jit(solution)/shard_map/ppermute | solution.py:236
  9.4 19.2 %collective-permute-start.7 = (bf16[32,4096]{1,0:T(8,128)(2,1)S(1)}, bf16[32,4096]{1,0:T(8,128)(2,1)S(1)}, u32[]{:S(2)}, u32[]{:S(2)}) collective-permute-start(bf16[32,4096]{1,0:T(8,128)(2,1)S(1)} %get-tuple-element.16.done), channel_id=1, source_target_pairs={{64,0},{65,1},{66,2},{67,3},{68,4},{69,5},{70,6},{71,7},{72,8},{73... | collective-permute-start | bytes 786440 | tf_op jit(solution)/shard_map/ppermute | solution.py:236
  15.3 13.3 %collective-permute-start.2 = (bf16[64,6144]{1,0:T(8,128)(2,1)S(1)}, bf16[64,6144]{1,0:T(8,128)(2,1)S(1)}, u32[]{:S(2)}, u32[]{:S(2)}) collective-permute-start(bf16[64,6144]{1,0:T(8,128)(2,1)S(1)} %get-tuple-element.20.sent), channel_id=1, source_target_pairs={{1,0},{0,1},{3,2},{2,3},{5,4},{4,5},{7,6},{6,7},{9,8},{8,9},{11,10... | collective-permute-start | bytes 2359304 | tf_op jit(solution)/shard_map/ppermute | solution.py:236
  18.3 13.2 %collective-permute-start.1 = (bf16[32,4096]{1,0:T(8,128)(2,1)S(1)}, bf16[32,4096]{1,0:T(8,128)(2,1)S(1)}, u32[]{:S(2)}, u32[]{:S(2)}) collective-permute-start(bf16[32,4096]{1,0:T(8,128)(2,1)S(1)} %after.6), channel_id=1, source_target_pairs={{4,0},{5,1},{6,2},{7,3},{8,4},{9,5},{10,6},{11,7},{12,8},{13,9},{1... | collective-permute-start | bytes 786440 | tf_op jit(solution)/shard_map/ppermute | solution.py:236
  24.7 18.7 %collective-permute-start.9 = (bf16[32,4096]{1,0:T(8,128)(2,1)S(1)}, bf16[32,4096]{1,0:T(8,128)(2,1)S(1)}, u32[]{:S(2)}, u32[]{:S(2)}) collective-permute-start(bf16[32,4096]{1,0:T(8,128)(2,1)S(1)} %after.7.done), channel_id=1, source_target_pairs={{64,0},{65,1},{66,2},{67,3},{68,4},{69,5},{70,6},{71,7},{72,8},{73... | collective-permute-start | bytes 786440 | tf_op jit(solution)/shard_map/ppermute | solution.py:236
  25.6 17.9 %collective-permute-start.5 = (bf16[32,4096]{1,0:T(8,128)(2,1)S(1)}, bf16[32,4096]{1,0:T(8,128)(2,1)S(1)}, u32[]{:S(2)}, u32[]{:S(2)}) collective-permute-start(bf16[32,4096]{1,0:T(8,128)(2,1)S(1)} %after.7.done), channel_id=1, source_target_pairs={{4,0},{5,1},{6,2},{7,3},{8,4},{9,5},{10,6},{11,7},{12,8},{13,9},{1... | collective-permute-start | bytes 786440 | tf_op jit(solution)/shard_map/ppermute | solution.py:236
  28.6 15.6 %collective-permute-start.8 = (bf16[32,4096]{1,0:T(8,128)(2,1)S(1)}, bf16[32,4096]{1,0:T(8,128)(2,1)S(1)}, u32[]{:S(2)}, u32[]{:S(2)}) collective-permute-start(bf16[32,4096]{1,0:T(8,128)(2,1)S(1)} %after.10.refs_0_), channel_id=1, source_target_pairs={{1,0},{0,1},{3,2},{2,3},{5,4},{4,5},{7,6},{6,7},{9,8},{8,9},{11,10... | collective-permute-start | bytes 786440 | tf_op jit(solution)/shard_map/ppermute | solution.py:236
  43.5 1.5 %collective-permute-start.10 = (bf16[32,4096]{1,0:T(8,128)(2,1)S(1)}, bf16[32,4096]{1,0:T(8,128)(2,1)S(1)}, u32[]{:S(2)}, u32[]{:S(2)}) collective-permute-start(bf16[32,4096]{1,0:T(8,128)(2,1)S(1)} %after.11.refs_2_), channel_id=1, source_target_pairs={{1,0},{0,1},{3,2},{2,3},{5,4},{4,5},{7,6},{6,7},{9,8},{8,9},{11,10... | collective-permute-start | bytes 786440 | tf_op jit(solution)/shard_map/ppermute | solution.py:236
  43.5 4.0 %collective-permute-start.6 = (bf16[32,4096]{1,0:T(8,128)(2,1)S(1)}, bf16[32,4096]{1,0:T(8,128)(2,1)S(1)}, u32[]{:S(2)}, u32[]{:S(2)}) collective-permute-start(bf16[32,4096]{1,0:T(8,128)(2,1)S(1)} %after.9.refs_2_), channel_id=1, source_target_pairs={{1,0},{0,1},{3,2},{2,3},{5,4},{4,5},{7,6},{6,7},{9,8},{8,9},{11,10... | collective-permute-start | bytes 786440 | tf_op jit(solution)/shard_map/ppermute | solution.py:236
  44.0 3.5 %collective-permute-start.4 = (bf16[32,4096]{1,0:T(8,128)(2,1)S(1)}, bf16[32,4096]{1,0:T(8,128)(2,1)S(1)}, u32[]{:S(2)}, u32[]{:S(2)}) collective-permute-start(bf16[32,4096]{1,0:T(8,128)(2,1)S(1)} %after.8.done.refs_0_), channel_id=1, source_target_pairs={{1,0},{0,1},{3,2},{2,3},{5,4},{4,5},{7,6},{6,7},{9,8},{8,9},{11,10... | collective-permute-start | bytes 786440 | tf_op jit(solution)/shard_map/ppermute | solution.py:236
  50.0 2.1 %collective-permute-start.13 = (bf16[32,2048]{1,0:T(8,128)(2,1)S(1)}, bf16[32,2048]{1,0:T(8,128)(2,1)S(1)}, u32[]{:S(2)}, u32[]{:S(2)}) collective-permute-start(bf16[32,2048]{1,0:T(8,128)(2,1)S(1)} %get-tuple-element.24), channel_id=1, source_target_pairs={{1,0},{0,1},{3,2},{2,3},{5,4},{4,5},{7,6},{6,7},{9,8},{8,9},{11,10... | collective-permute-start | bytes 393224 | tf_op jit(solution)/shard_map/ppermute | solution.py:236
  50.2 12.8 %collective-permute-start.12 = (f32[32,2048]{1,0:T(8,128)S(1)}, f32[32,2048]{1,0:T(8,128)S(1)}, u32[]{:S(2)}, u32[]{:S(2)}) collective-permute-start(f32[32,2048]{1,0:T(8,128)S(1)} %get-tuple-element.23), channel_id=1, source_target_pairs={{1,0},{0,1},{3,2},{2,3},{5,4},{4,5},{7,6},{6,7},{9,8},{8,9},{11,10... | collective-permute-start | bytes 786440 | tf_op jit(solution)/shard_map/ppermute | solution.py:236
  50.6 10.2 %collective-permute-start.11 = (bf16[32,2048]{1,0:T(8,128)(2,1)S(1)}, bf16[32,2048]{1,0:T(8,128)(2,1)S(1)}, u32[]{:S(2)}, u32[]{:S(2)}) collective-permute-start(bf16[32,2048]{1,0:T(8,128)(2,1)S(1)} %get-tuple-element.22), channel_id=1, source_target_pairs={{2,0},{3,1},{0,2},{1,3},{6,4},{7,5},{4,6},{5,7},{10,8},{11,9},{8,1... | collective-permute-start | bytes 393224 | tf_op jit(solution)/shard_map/ppermute | solution.py:236
  52.1 10.9 %collective-permute-start.14 = (bf16[32,2048]{1,0:T(8,128)(2,1)S(1)}, bf16[32,2048]{1,0:T(8,128)(2,1)S(1)}, u32[]{:S(2)}, u32[]{:S(2)}) collective-permute-start(bf16[32,2048]{1,0:T(8,128)(2,1)S(1)} %collective-permute-done.13), channel_id=1, source_target_pairs={{2,0},{3,1},{0,2},{1,3},{6,4},{7,5},{4,6},{5,7},{10,8},{11,9},{8,1... | collective-permute-start | bytes 393224 | tf_op jit(solution)/shard_map/ppermute | solution.py:236

commit v2 on v1

--- a/solution.py
+++ b/solution.py
@@ -195,29 +195,26 @@
 def finish_kernel(core, *refs):
     parts, out, held = refs[:-2], refs[-2], refs[-1]
     half = core[0]
-    per = 16
+    own, zed, other, diag = parts
+    rows = pl.ds(pl.multiple_of(pl.program_id(0) * 16, 16), 16)
     for ap in range(16):
-        own, zed, other, diag = parts[ap // per * 4 : ap // per * 4 + 4]
-        at = slice(ap % per * 128, (ap % per + 1) * 128)
-        held[pl.ds(half * 16 + ap, 32, stride=32), :] = own[:, at] + zed[:, at].astype(F32)
-        held[pl.ds((1 - half) * 16 + ap, 32, stride=32), :] = other[:, at] + diag[:, at].astype(F32)
-
-    def put(n, _):
-        x = held[pl.ds(pl.multiple_of(n * 32, 32), 32), :]
+        at = slice(ap * 128, (ap + 1) * 128)
+        held[pl.ds(half * 16 + ap, 16, stride=32), :] = own[rows, at] + zed[rows, at].astype(F32)
+        held[pl.ds((1 - half) * 16 + ap, 16, stride=32), :] = other[rows, at] + diag[rows, at].astype(F32)
+    for n in range(16):
+        x = held[n * 32 : (n + 1) * 32, :]
         out[n, 0:32, :] = x[:, :64]
         out[n, 32:64, :] = x[:, 64:]
-        return 0
-
-    lax.fori_loop(0, 32, put, 0, unroll=16)
 
 
 def finish(core, parts):
     return pl.pallas_call(
         finish_kernel,
+        grid=(2,),
         out_shape=jax.ShapeDtypeStruct((32, 64, 64), F32),
         in_specs=[SMEM] + [VMEM] * len(parts),
-        out_specs=VMEM,
-        scratch_shapes=[pltpu.VMEM((1024, 128), F32)],
+        out_specs=pl.BlockSpec((16, 64, 64), lambda i: (i, 0, 0)),
+        scratch_shapes=[pltpu.VMEM((512, 128), F32)],
         compiler_params=params(8),
         cost_estimate=cost(0, 6),
         name="finish",

time: 64.9 us -> 64.7 us (level)
  no operation moved by 1% of the time
where the time goes in v2:
time: 64.7 us; the launch traced here: 64.5 us
  Pallas kernels  25.8 us (40%)
  starting transfers between devices  22.2 us (34%)
  waiting for transfers between devices  16.3 us (25%)
    ppermute x15, starting transfers between devices, moved(): return lax.ppermute(x, AXES, route)  22.2 us
    ppermute x15, waiting for transfers between devices, moved(): return lax.ppermute(x, AXES, route)  16.3 us
    pallas_call x4, Pallas kernels, build(): pl.pallas_call(functools.partial(build_kernel, first), out_shape=pltpu.VM...  11.5 us
    pallas_call x2, Pallas kernels, flat_factors(): pl.pallas_call(factor_kernel, grid=(2,), out_shape=[jax.ShapeDtypeStruct(...  6.19 us
    pallas_call x2, Pallas kernels, contract(): pl.pallas_call(functools.partial(contract_kernel, last, first), out_shape...  4.93 us
    pallas_call x1, Pallas kernels, flat_lambda(): pl.pallas_call(lambda_kernel, grid=(1,), out_shape=[jax.ShapeDtypeStruct(...  1.63 us
    pallas_call x1, Pallas kernels, finish(): pl.pallas_call(finish_kernel, grid=(2,), out_shape=jax.ShapeDtypeStruct((...  1.52 us
  transfers between devices with their start and end apart: 15, of which 4 were waited for; matrix products, arithmetic and copies ran while one was open for 0% of the time, Pallas kernels for 26%

profile of v2, /device:TPU:96, one launch (start us, length us, event | category | flops | bytes accessed | tf_op | source)
XLA Modules:
  0.0 64.5 jit_solution(11801012056371825218)
XLA Ops:
  0.0 1.6 %flat_lambda.1 = (bf16[32,4096]{1,0:T(8,128)(2,1)S(1)}, bf16[32,4096]{1,0:T(8,128)(2,1)S(1)}) custom-call(bf16[32,64,64]{2,1,0:T(8,128)(2,1)} %bitcast.9), custom_call_target="tpu_custom_call" | custom-call | bytes 6144 | tf_op jit(solution)/shard_map/flat_lambda/pallas_call | solution.py:59
  1.6 3.1 %flat_factors.2 = (bf16[64,2048]{1,0:T(8,128)(2,1)S(1)}, bf16[64,6144]{1,0:T(8,128)(2,1)S(1)}) custom-call(s32[1]{0:T(128)} %bitcast.core, bf16[2,64,64,64]{3,2,1,0:T(8,128)(2,1)} %bitcast.5, bf16[2,64,64,64]{3,2,1,0:T(8,128)(2,1)} %bitcast.7, bf16[32,4096]{1,0:T(8,128)(2,1)S(1)} %get-tuple-element.16.done), custom_call_target="tpu_custom_call" | custom-call | bytes 409600000 | tf_op jit(solution)/shard_map/flat_factors/pallas_call | solution.py:80
  4.9 4.6 %collective-permute-start.3 = (bf16[32,4096]{1,0:T(8,128)(2,1)S(1)}, bf16[32,4096]{1,0:T(8,128)(2,1)S(1)}, u32[]{:S(2)}, u32[]{:S(2)}) collective-permute-start(bf16[32,4096]{1,0:T(8,128)(2,1)S(1)} %get-tuple-element.16.done), channel_id=1, source_target_pairs={{2,0},{3,1},{0,2},{1,3},{6,4},{7,5},{4,6},{5,7},{10,8},{11,9},{8,1... | collective-permute-start | bytes 786440 | tf_op jit(solution)/shard_map/ppermute | solution.py:233
  9.4 2.8 %collective-permute-start.7 = (bf16[32,4096]{1,0:T(8,128)(2,1)S(1)}, bf16[32,4096]{1,0:T(8,128)(2,1)S(1)}, u32[]{:S(2)}, u32[]{:S(2)}) collective-permute-start(bf16[32,4096]{1,0:T(8,128)(2,1)S(1)} %get-tuple-element.16.done), channel_id=1, source_target_pairs={{64,0},{65,1},{66,2},{67,3},{68,4},{69,5},{70,6},{71,7},{72,8},{73... | collective-permute-start | bytes 786440 | tf_op jit(solution)/shard_map/ppermute | solution.py:233
  12.2 3.1 %flat_factors.3 = (bf16[64,2048]{1,0:T(8,128)(2,1)S(1)}, bf16[64,6144]{1,0:T(8,128)(2,1)S(1)}) custom-call(s32[1]{0:T(128)} %bitcast.core, bf16[2,64,64,64]{3,2,1,0:T(8,128)(2,1)} %bitcast.6, bf16[2,64,64,64]{3,2,1,0:T(8,128)(2,1)} %bitcast.8, bf16[64,2048]{1,0:T(8,128)(2,1)S(1)} %get-tuple-element.17.done.mine), custom_call_target="tpu_custom_call" | custom-call | bytes 409600000 | tf_op jit(solution)/shard_map/flat_factors/pallas_call | solution.py:80
  15.4 2.9 %build_w.4.done.refs_4_ = bf16[2048,2048]{1,0:T(8,128)(2,1)S(1)} custom-call(bf16[64,2048]{1,0:T(8,128)(2,1)S(1)} %get-tuple-element.17.done.mine, bf16[64,6144]{1,0:T(8,128)(2,1)S(1)} %get-tuple-element.18.sent, bf16[64,6144]{1,0:T(8,128)(2,1)S(1)} %collective-permute-done.got_here, bf16[64,2048]{1,0:T(8,128)(2,1)S(1)} %get-tuple-element.19.done.mine), custom_call_target="tpu_custom_call" | custom-call | flops 2147483 | bytes 9216 | tf_op jit(solution)/shard_map/build_w/pallas_call | solution.py:140
  18.3 3.5 %collective-permute-start.1 = (bf16[32,4096]{1,0:T(8,128)(2,1)S(1)}, bf16[32,4096]{1,0:T(8,128)(2,1)S(1)}, u32[]{:S(2)}, u32[]{:S(2)}) collective-permute-start(bf16[32,4096]{1,0:T(8,128)(2,1)S(1)} %after.6), channel_id=1, source_target_pairs={{4,0},{5,1},{6,2},{7,3},{8,4},{9,5},{10,6},{11,7},{12,8},{13,9},{1... | collective-permute-start | bytes 786440 | tf_op jit(solution)/shard_map/ppermute | solution.py:233
  21.8 2.9 %build_w.5.done.refs_5_ = bf16[2048,2048]{1,0:T(8,128)(2,1)S(1)} custom-call(bf16[64,2048]{1,0:T(8,128)(2,1)S(1)} %get-tuple-element.17.done.mine, bf16[64,6144]{1,0:T(8,128)(2,1)S(1)} %get-tuple-element.18.sent, bf16[64,6144]{1,0:T(8,128)(2,1)S(1)} %collective-permute-done.got_here, bf16[2048,2048]{1,0:T(8,128)(2,1)S(1)} %build_w.4.done.refs_4_), custom_call_target="tpu_custom_call" | custom-call | flops 85899345920 | bytes 368640000 | tf_op jit(solution)/shard_map/build_w/pallas_call | solution.py:140
  24.7 0.9 %collective-permute-start.9 = (bf16[32,4096]{1,0:T(8,128)(2,1)S(1)}, bf16[32,4096]{1,0:T(8,128)(2,1)S(1)}, u32[]{:S(2)}, u32[]{:S(2)}) collective-permute-start(bf16[32,4096]{1,0:T(8,128)(2,1)S(1)} %after.7.done), channel_id=1, source_target_pairs={{64,0},{65,1},{66,2},{67,3},{68,4},{69,5},{70,6},{71,7},{72,8},{73... | collective-permute-start | bytes 786440 | tf_op jit(solution)/shard_map/ppermute | solution.py:233
  25.6 3.0 %collective-permute-start.5 = (bf16[32,4096]{1,0:T(8,128)(2,1)S(1)}, bf16[32,4096]{1,0:T(8,128)(2,1)S(1)}, u32[]{:S(2)}, u32[]{:S(2)}) collective-permute-start(bf16[32,4096]{1,0:T(8,128)(2,1)S(1)} %after.7.done), channel_id=1, source_target_pairs={{4,0},{5,1},{6,2},{7,3},{8,4},{9,5},{10,6},{11,7},{12,8},{13,9},{1... | collective-permute-start | bytes 786440 | tf_op jit(solution)/shard_map/ppermute | solution.py:233
  28.6 2.9 %build_w.6.done.refs_4_ = bf16[2048,2048]{1,0:T(8,128)(2,1)S(1)} custom-call(bf16[64,2048]{1,0:T(8,128)(2,1)S(1)} %get-tuple-element.19.done.mine, bf16[64,6144]{1,0:T(8,128)(2,1)S(1)} %get-tuple-element.20.sent, bf16[64,6144]{1,0:T(8,128)(2,1)S(1)} %collective-permute-done.2.got_here, bf16[32,4096]{1,0:T(8,128)(2,1)S(1)} %after.7.done), custom_call_target="tpu_custom_call" | custom-call | flops 2147483 | bytes 9216 | tf_op jit(solution)/shard_map/build_w/pallas_call | solution.py:140
  31.5 2.9 %build_w.7.done.refs_5_ = bf16[2048,2048]{1,0:T(8,128)(2,1)S(1)} custom-call(bf16[64,2048]{1,0:T(8,128)(2,1)S(1)} %get-tuple-element.19.done.mine, bf16[64,6144]{1,0:T(8,128)(2,1)S(1)} %get-tuple-element.20.sent, bf16[64,6144]{1,0:T(8,128)(2,1)S(1)} %collective-permute-done.2.got_here, bf16[32,4096]{1,0:T(8,128)(2,1)S(1)} %after.8.done.refs_0_), custom_call_target="tpu_custom_call" | custom-call | flops 2147483 | bytes 9216 | tf_op jit(solution)/shard_map/build_w/pallas_call | solution.py:140
  34.4 9.0 %collective-permute-done.9.x = bf16[32,4096]{1,0:T(8,128)(2,1)S(1)} collective-permute-done((bf16[32,4096]{1,0:T(8,128)(2,1)S(1)}, bf16[32,4096]{1,0:T(8,128)(2,1)S(1)}, u32[]{:S(2)}, u32[]{:S(2)}) %collective-permute-start.9) | collective-permute-done | bytes 262176 | tf_op jit(solution)/shard_map/ppermute | solution.py:233
  43.5 0.5 collective-permute-start.6
  44.2 0.8 %collective-permute-done.10.refs_3_ = bf16[32,4096]{1,0:T(8,128)(2,1)S(1)} collective-permute-done((bf16[32,4096]{1,0:T(8,128)(2,1)S(1)}, bf16[32,4096]{1,0:T(8,128)(2,1)S(1)}, u32[]{:S(2)}, u32[]{:S(2)}) %collective-permute-start.10) | collective-permute-done | bytes 262176 | tf_op jit(solution)/shard_map/ppermute | solution.py:233
  45.0 2.5 %contract.2.refs_6_ = f32[128,2048]{1,0:T(8,128)S(1)} custom-call(bf16[32,4096]{1,0:T(8,128)(2,1)S(1)} %after.10.refs_0_, bf16[32,4096]{1,0:T(8,128)(2,1)S(1)} %collective-permute-done.8.refs_1_, bf16[32,4096]{1,0:T(8,128)(2,1)S(1)} %after.11.refs_2_, bf16[32,4096]{1,0:T(8,128)(2,1)S(1)} %collective-permute-done.10.refs_3_, ...), custom_call_target="tpu_custom_call" | custom-call | flops 2147483 | bytes 12288 | tf_op jit(solution)/shard_map/contract/pallas_call | solution.py:183
  47.5 2.5 %contract.3 = (f32[32,2048]{1,0:T(8,128)S(1)}, f32[32,2048]{1,0:T(8,128)S(1)}, bf16[32,2048]{1,0:T(8,128)(2,1)S(1)}, bf16[32,2048]{1,0:T(8,128)(2,1)S(1)}) custom-call(bf16[32,4096]{1,0:T(8,128)(2,1)S(1)} %after.8.done.refs_0_, bf16[32,4096]{1,0:T(8,128)(2,1)S(1)} %collective-permute-done.4.refs_1_, bf16[32,4096]{1,0:T(8,128)(2,1)S(1)} %after.9.refs_2_, ...), custom_call_target="tpu_custom_call" | custom-call | flops 2147483 | bytes 12288 | tf_op jit(solution)/shard_map/contract/pallas_call | solution.py:183
  50.0 0.2 collective-permute-start.13
  50.2 0.4 collective-permute-start.12
  50.6 1.5 %collective-permute-start.11 = (bf16[32,2048]{1,0:T(8,128)(2,1)S(1)}, bf16[32,2048]{1,0:T(8,128)(2,1)S(1)}, u32[]{:S(2)}, u32[]{:S(2)}) collective-permute-start(bf16[32,2048]{1,0:T(8,128)(2,1)S(1)} %get-tuple-element.22), channel_id=1, source_target_pairs={{2,0},{3,1},{0,2},{1,3},{6,4},{7,5},{4,6},{5,7},{10,8},{11,9},{8,1... | collective-permute-start | bytes 393224 | tf_op jit(solution)/shard_map/ppermute | solution.py:233
  52.1 4.4 %collective-permute-start.14 = (bf16[32,2048]{1,0:T(8,128)(2,1)S(1)}, bf16[32,2048]{1,0:T(8,128)(2,1)S(1)}, u32[]{:S(2)}, u32[]{:S(2)}) collective-permute-start(bf16[32,2048]{1,0:T(8,128)(2,1)S(1)} %collective-permute-done.13), channel_id=1, source_target_pairs={{2,0},{3,1},{0,2},{1,3},{6,4},{7,5},{4,6},{5,7},{10,8},{11,9},{8,1... | collective-permute-start | bytes 393224 | tf_op jit(solution)/shard_map/ppermute | solution.py:233
  56.5 4.3 %collective-permute-done.11.refs_1_ = bf16[32,2048]{1,0:T(8,128)(2,1)S(1)} collective-permute-done((bf16[32,2048]{1,0:T(8,128)(2,1)S(1)}, bf16[32,2048]{1,0:T(8,128)(2,1)S(1)}, u32[]{:S(2)}, u32[]{:S(2)}) %collective-permute-start.11) | collective-permute-done | bytes 131104 | tf_op jit(solution)/shard_map/ppermute | solution.py:233
  60.8 2.2 %collective-permute-done.14.refs_3_ = bf16[32,2048]{1,0:T(8,128)(2,1)S(1)} collective-permute-done((bf16[32,2048]{1,0:T(8,128)(2,1)S(1)}, bf16[32,2048]{1,0:T(8,128)(2,1)S(1)}, u32[]{:S(2)}, u32[]{:S(2)}) %collective-permute-start.14) | collective-permute-done | bytes 131104 | tf_op jit(solution)/shard_map/ppermute | solution.py:233
  63.0 1.5 %finish.1 = f32[32,64,64]{2,1,0:T(8,128)} custom-call(s32[1]{0:T(128)} %bitcast.core, f32[32,2048]{1,0:T(8,128)S(1)} %get-tuple-element.21.refs_0_, bf16[32,2048]{1,0:T(8,128)(2,1)S(1)} %collective-permute-done.11.refs_1_, f32[32,2048]{1,0:T(8,128)S(1)} %collective-permute-done.12.refs_2_, bf16[32,2048]{1,0:T(8,128)(2,1)S(1)} %collective-permute-done.14.refs_3_), custom_call_target="tpu_custom_call" | custom-call | bytes 6144 | tf_op jit(solution)/shard_map/finish/pallas_call | solution.py:211
  (22 shorter events, 0.5 us)
Async XLA Ops:
  4.8 10.6 %collective-permute-start = (bf16[64,6144]{1,0:T(8,128)(2,1)S(1)}, bf16[64,6144]{1,0:T(8,128)(2,1)S(1)}, u32[]{:S(2)}, u32[]{:S(2)}) collective-permute-start(bf16[64,6144]{1,0:T(8,128)(2,1)S(1)} %get-tuple-element.18.sent), channel_id=1, source_target_pairs={{1,0},{0,1},{3,2},{2,3},{5,4},{4,5},{7,6},{6,7},{9,8},{8,9},{11,10... | collective-permute-start | bytes 2359304 | tf_op jit(solution)/shard_map/ppermute | solution.py:233
  4.9 19.9 %collective-permute-start.3 = (bf16[32,4096]{1,0:T(8,128)(2,1)S(1)}, bf16[32,4096]{1,0:T(8,128)(2,1)S(1)}, u32[]{:S(2)}, u32[]{:S(2)}) collective-permute-start(bf16[32,4096]{1,0:T(8,128)(2,1)S(1)} %get-tuple-element.16.done), channel_id=1, source_target_pairs={{2,0},{3,1},{0,2},{1,3},{6,4},{7,5},{4,6},{5,7},{10,8},{11,9},{8,1... | collective-permute-start | bytes 786440 | tf_op jit(solution)/shard_map/ppermute | solution.py:233
  9.4 19.2 %collective-permute-start.7 = (bf16[32,4096]{1,0:T(8,128)(2,1)S(1)}, bf16[32,4096]{1,0:T(8,128)(2,1)S(1)}, u32[]{:S(2)}, u32[]{:S(2)}) collective-permute-start(bf16[32,4096]{1,0:T(8,128)(2,1)S(1)} %get-tuple-element.16.done), channel_id=1, source_target_pairs={{64,0},{65,1},{66,2},{67,3},{68,4},{69,5},{70,6},{71,7},{72,8},{73... | collective-permute-start | bytes 786440 | tf_op jit(solution)/shard_map/ppermute | solution.py:233
  15.3 13.3 %collective-permute-start.2 = (bf16[64,6144]{1,0:T(8,128)(2,1)S(1)}, bf16[64,6144]{1,0:T(8,128)(2,1)S(1)}, u32[]{:S(2)}, u32[]{:S(2)}) collective-permute-start(bf16[64,6144]{1,0:T(8,128)(2,1)S(1)} %get-tuple-element.20.sent), channel_id=1, source_target_pairs={{1,0},{0,1},{3,2},{2,3},{5,4},{4,5},{7,6},{6,7},{9,8},{8,9},{11,10... | collective-permute-start | bytes 2359304 | tf_op jit(solution)/shard_map/ppermute | solution.py:233
  18.3 13.2 %collective-permute-start.1 = (bf16[32,4096]{1,0:T(8,128)(2,1)S(1)}, bf16[32,4096]{1,0:T(8,128)(2,1)S(1)}, u32[]{:S(2)}, u32[]{:S(2)}) collective-permute-start(bf16[32,4096]{1,0:T(8,128)(2,1)S(1)} %after.6), channel_id=1, source_target_pairs={{4,0},{5,1},{6,2},{7,3},{8,4},{9,5},{10,6},{11,7},{12,8},{13,9},{1... | collective-permute-start | bytes 786440 | tf_op jit(solution)/shard_map/ppermute | solution.py:233
  24.7 18.7 %collective-permute-start.9 = (bf16[32,4096]{1,0:T(8,128)(2,1)S(1)}, bf16[32,4096]{1,0:T(8,128)(2,1)S(1)}, u32[]{:S(2)}, u32[]{:S(2)}) collective-permute-start(bf16[32,4096]{1,0:T(8,128)(2,1)S(1)} %after.7.done), channel_id=1, source_target_pairs={{64,0},{65,1},{66,2},{67,3},{68,4},{69,5},{70,6},{71,7},{72,8},{73... | collective-permute-start | bytes 786440 | tf_op jit(solution)/shard_map/ppermute | solution.py:233
  25.6 17.9 %collective-permute-start.5 = (bf16[32,4096]{1,0:T(8,128)(2,1)S(1)}, bf16[32,4096]{1,0:T(8,128)(2,1)S(1)}, u32[]{:S(2)}, u32[]{:S(2)}) collective-permute-start(bf16[32,4096]{1,0:T(8,128)(2,1)S(1)} %after.7.done), channel_id=1, source_target_pairs={{4,0},{5,1},{6,2},{7,3},{8,4},{9,5},{10,6},{11,7},{12,8},{13,9},{1... | collective-permute-start | bytes 786440 | tf_op jit(solution)/shard_map/ppermute | solution.py:233
  28.6 15.6 %collective-permute-start.8 = (bf16[32,4096]{1,0:T(8,128)(2,1)S(1)}, bf16[32,4096]{1,0:T(8,128)(2,1)S(1)}, u32[]{:S(2)}, u32[]{:S(2)}) collective-permute-start(bf16[32,4096]{1,0:T(8,128)(2,1)S(1)} %after.10.refs_0_), channel_id=1, source_target_pairs={{1,0},{0,1},{3,2},{2,3},{5,4},{4,5},{7,6},{6,7},{9,8},{8,9},{11,10... | collective-permute-start | bytes 786440 | tf_op jit(solution)/shard_map/ppermute | solution.py:233
  43.5 1.5 %collective-permute-start.10 = (bf16[32,4096]{1,0:T(8,128)(2,1)S(1)}, bf16[32,4096]{1,0:T(8,128)(2,1)S(1)}, u32[]{:S(2)}, u32[]{:S(2)}) collective-permute-start(bf16[32,4096]{1,0:T(8,128)(2,1)S(1)} %after.11.refs_2_), channel_id=1, source_target_pairs={{1,0},{0,1},{3,2},{2,3},{5,4},{4,5},{7,6},{6,7},{9,8},{8,9},{11,10... | collective-permute-start | bytes 786440 | tf_op jit(solution)/shard_map/ppermute | solution.py:233
  43.5 4.0 %collective-permute-start.6 = (bf16[32,4096]{1,0:T(8,128)(2,1)S(1)}, bf16[32,4096]{1,0:T(8,128)(2,1)S(1)}, u32[]{:S(2)}, u32[]{:S(2)}) collective-permute-start(bf16[32,4096]{1,0:T(8,128)(2,1)S(1)} %after.9.refs_2_), channel_id=1, source_target_pairs={{1,0},{0,1},{3,2},{2,3},{5,4},{4,5},{7,6},{6,7},{9,8},{8,9},{11,10... | collective-permute-start | bytes 786440 | tf_op jit(solution)/shard_map/ppermute | solution.py:233
  44.0 3.5 %collective-permute-start.4 = (bf16[32,4096]{1,0:T(8,128)(2,1)S(1)}, bf16[32,4096]{1,0:T(8,128)(2,1)S(1)}, u32[]{:S(2)}, u32[]{:S(2)}) collective-permute-start(bf16[32,4096]{1,0:T(8,128)(2,1)S(1)} %after.8.done.refs_0_), channel_id=1, source_target_pairs={{1,0},{0,1},{3,2},{2,3},{5,4},{4,5},{7,6},{6,7},{9,8},{8,9},{11,10... | collective-permute-start | bytes 786440 | tf_op jit(solution)/shard_map/ppermute | solution.py:233
  50.0 2.1 %collective-permute-start.13 = (bf16[32,2048]{1,0:T(8,128)(2,1)S(1)}, bf16[32,2048]{1,0:T(8,128)(2,1)S(1)}, u32[]{:S(2)}, u32[]{:S(2)}) collective-permute-start(bf16[32,2048]{1,0:T(8,128)(2,1)S(1)} %get-tuple-element.24), channel_id=1, source_target_pairs={{1,0},{0,1},{3,2},{2,3},{5,4},{4,5},{7,6},{6,7},{9,8},{8,9},{11,10... | collective-permute-start | bytes 393224 | tf_op jit(solution)/shard_map/ppermute | solution.py:233
  50.2 12.8 %collective-permute-start.12 = (f32[32,2048]{1,0:T(8,128)S(1)}, f32[32,2048]{1,0:T(8,128)S(1)}, u32[]{:S(2)}, u32[]{:S(2)}) collective-permute-start(f32[32,2048]{1,0:T(8,128)S(1)} %get-tuple-element.23), channel_id=1, source_target_pairs={{1,0},{0,1},{3,2},{2,3},{5,4},{4,5},{7,6},{6,7},{9,8},{8,9},{11,10... | collective-permute-start | bytes 786440 | tf_op jit(solution)/shard_map/ppermute | solution.py:233
  50.6 10.2 %collective-permute-start.11 = (bf16[32,2048]{1,0:T(8,128)(2,1)S(1)}, bf16[32,2048]{1,0:T(8,128)(2,1)S(1)}, u32[]{:S(2)}, u32[]{:S(2)}) collective-permute-start(bf16[32,2048]{1,0:T(8,128)(2,1)S(1)} %get-tuple-element.22), channel_id=1, source_target_pairs={{2,0},{3,1},{0,2},{1,3},{6,4},{7,5},{4,6},{5,7},{10,8},{11,9},{8,1... | collective-permute-start | bytes 393224 | tf_op jit(solution)/shard_map/ppermute | solution.py:233
  52.1 10.9 %collective-permute-start.14 = (bf16[32,2048]{1,0:T(8,128)(2,1)S(1)}, bf16[32,2048]{1,0:T(8,128)(2,1)S(1)}, u32[]{:S(2)}, u32[]{:S(2)}) collective-permute-start(bf16[32,2048]{1,0:T(8,128)(2,1)S(1)} %collective-permute-done.13), channel_id=1, source_target_pairs={{2,0},{3,1},{0,2},{1,3},{6,4},{7,5},{4,6},{5,7},{10,8},{11,9},{8,1... | collective-permute-start | bytes 393224 | tf_op jit(solution)/shard_map/ppermute | solution.py:233
